TPU v7x, 128 devices: a whole 4x4x4 slice. The times are simulated.
128 devices in a mesh: dp: 16 (over y, x), tensor: 8 (over z, core).
Axes of the slice: x: 4, y: 4, z: 4, core: 2. Of those that a mesh axis runs over, the one named last changes fastest.
Arguments:
- queries: bfloat16 [256, 64, 8192], P('dp', None, 'tensor'), may hold values from -10 to 50
- fresh_kv: bfloat16 [256, 2, 64, 1024], P('dp', None, None, 'tensor'), may hold values from -6 to 7.5
- kv_cache: bfloat16 [256, 2, 512, 1024], P('dp', None, None, 'tensor'), may hold values from -6 to 7.5
- parent_device: int32 [256, 1], P('dp'), may hold values from 0 to 15; in each aligned block of 16 rows (0 to 15, 16 to 31, ...) at most 2 rows name the same one
- parent_rank: int32 [256], P('dp'), may hold values from 0 to 1
- cache_length: int32 [8], replicated, may hold values from 1 to 512, 2560 in all
- out_weight: bfloat16 [8192, 8192], P('tensor'), may hold values from -1 to 1
- residual: bfloat16 [256, 64, 8192], P('dp', None, 'tensor'), may hold values from -132 to 132
- norm_gain: bfloat16 [8192], P('tensor'), may hold values from 0.25 to 1.75
Outputs:
- normed: bfloat16 [256, 64, 8192], P('dp', None, 'tensor')
Inputs may be any that keep to these rules, and one draw needn't show every extreme that they name: `parent_device`: among the 16 beams of one dp index, at most 2 have their parent on the same dp index, and in every draw some dp index has exactly 2 parents on one dp index. `cache_length`: some problem has exactly 512 live positions in every draw.
All inputs are finite; a program needn't handle non-finite values.
Results may differ from a plain program's by a relative error of at most 0.015.
Values may be sent and summed in bfloat16 or wider, within the bound.
A program may use at most 192 MiB of HBM per device.

v0:
```python
import math

import jax
import jax.numpy as jnp
from jax import lax
from jax.sharding import PartitionSpec as P

D = 8192
HEAD = 128
QPK = 8


epsilon = 1e-06


def attend(queries, fresh_kv, kv_cache, lengths):
    beam_count = queries.shape[0]
    step_count = queries.shape[1]
    cache_positions = kv_cache.shape[2]
    kv_heads = fresh_kv.shape[3] // HEAD
    scaling = 1.0 / math.sqrt(HEAD)
    grouped = queries.reshape(beam_count, step_count, kv_heads, QPK, HEAD)
    cached_keys = kv_cache[:, 0].reshape(beam_count, cache_positions, kv_heads, HEAD)
    cached_values = kv_cache[:, 1].reshape(beam_count, cache_positions, kv_heads, HEAD)
    fresh_keys = fresh_kv[:, 0].reshape(beam_count, step_count, kv_heads, HEAD)
    fresh_values = fresh_kv[:, 1].reshape(beam_count, step_count, kv_heads, HEAD)
    cache_scores = (
        jnp.einsum("bsngd,btnd->bngst", grouped, cached_keys, preferred_element_type=jnp.float32)
        * scaling
    )
    fresh_scores = (
        jnp.einsum("bsngd,bund->bngsu", grouped, fresh_keys, preferred_element_type=jnp.float32)
        * scaling
    )
    live_mask = (jnp.arange(cache_positions, dtype=jnp.int32)[None, :] < lengths[:, None]).reshape(
        beam_count, 1, 1, 1, cache_positions
    )
    causal_mask = (
        jnp.arange(step_count, dtype=jnp.int32)[:, None]
        >= jnp.arange(step_count, dtype=jnp.int32)[None, :]
    )
    cache_scores = jnp.where(live_mask, cache_scores, -jnp.inf)
    fresh_scores = jnp.where(causal_mask, fresh_scores, -jnp.inf)
    highest = jnp.maximum(jnp.max(cache_scores, axis=-1), jnp.max(fresh_scores, axis=-1))[..., None]
    cache_probs = jnp.exp(cache_scores - highest)
    fresh_probs = jnp.exp(fresh_scores - highest)
    denominator = jnp.sum(cache_probs, axis=-1, keepdims=True) + jnp.sum(
        fresh_probs, axis=-1, keepdims=True
    )
    cache_weights = (cache_probs / denominator).astype(jnp.bfloat16)
    fresh_weights = (fresh_probs / denominator).astype(jnp.bfloat16)
    combined = jnp.einsum(
        "bngst,btnd->bsngd", cache_weights, cached_values, preferred_element_type=jnp.float32
    )
    combined = combined + jnp.einsum(
        "bngsu,bund->bsngd", fresh_weights, fresh_values, preferred_element_type=jnp.float32
    )
    return combined.astype(jnp.bfloat16).reshape(beam_count, step_count, kv_heads * QPK * HEAD)


def pick_length(slot_list, cache_length):
    problems = cache_length.shape[0]
    match_table = (slot_list % problems)[:, None] == jnp.arange(problems, dtype=jnp.int32)[None, :]
    return jnp.sum(jnp.where(match_table, cache_length[None, :], 0), axis=1)


def on_device(
    queries,
    fresh_kv,
    kv_cache,
    parent_device,
    parent_rank,
    cache_length,
    out_weight,
    residual,
    norm_gain,
):
    devices = lax.axis_size("dp")
    beam_count = queries.shape[0]
    step_count = queries.shape[1]
    width_query = queries.shape[2]
    capacity = max(2, 2 * beam_count // devices)
    problems = cache_length.shape[0]
    source = parent_device[:, 0]
    slot_ids = jnp.arange(beam_count, dtype=jnp.int32)
    parent_slot = parent_rank * problems + slot_ids % problems
    onehot = (source[:, None] == jnp.arange(devices, dtype=jnp.int32)[None, :]).astype(jnp.int32)
    earlier = jnp.cumsum(onehot, axis=0) - onehot
    position = jnp.sum(earlier * onehot, axis=1)
    picked = source * capacity + position
    request = jnp.zeros((devices, capacity), jnp.int32).at[source, position].set(parent_slot)
    asked_slots = lax.all_to_all(request, "dp", split_axis=0, concat_axis=0, tiled=True)
    outgoing = jnp.take(kv_cache, asked_slots.reshape(-1), axis=0).reshape(
        (devices, capacity) + kv_cache.shape[1:]
    )
    arrived = lax.all_to_all(outgoing, "dp", split_axis=0, concat_axis=0, tiled=True)
    flattened = arrived.reshape((devices * capacity,) + kv_cache.shape[1:])
    inherited = jnp.take(flattened, picked, axis=0)
    mixed_heads = attend(queries, fresh_kv, inherited, pick_length(slot_ids, cache_length))
    row_total = beam_count * step_count
    partial_terms = jnp.dot(
        mixed_heads.reshape(row_total, width_query), out_weight, preferred_element_type=jnp.float32
    )
    shared = lax.psum_scatter(
        partial_terms.astype(jnp.bfloat16), "tensor", scatter_dimension=1, tiled=True
    ).astype(jnp.float32)
    attended = residual.reshape(row_total, residual.shape[2]).astype(jnp.float32) + shared
    squares = lax.psum(jnp.sum(attended * attended, axis=1), "tensor")
    normed = (
        attended
        * lax.rsqrt(squares / D + epsilon)[:, None]
        * norm_gain.astype(jnp.float32)[None, :]
    )
    return normed.astype(jnp.bfloat16).reshape(beam_count, step_count, residual.shape[2])


def solution(mesh):
    placed = (
        P("dp", None, "tensor"),
        P("dp", None, None, "tensor"),
        P("dp", None, None, "tensor"),
        P("dp", None),
        P("dp"),
        P(),
        P("tensor", None),
        P("dp", None, "tensor"),
        P("tensor"),
    )
    return jax.shard_map(
        on_device, mesh=mesh, in_specs=placed, out_specs=P("dp", None, "tensor"), check_vma=False
    )
```

profile of v0, /device:TPU:1, one launch (start us, length us, event | category | flops | bytes accessed | tf_op | source)
XLA Modules:
  0.0 353.9 jit_solution(14915801227543439040)
XLA Ops:
  6.5 0.0 copy-start
  6.5 0.9 fusion.28
  7.4 0.8 select_reduce_fusion
  8.3 0.7 fusion.31
  9.0 0.7 multiply_add_fusion
  9.6 1.3 scatter_fusion
  10.9 0.1 copy.36
  11.0 13.8 %all_to_all.14 = s32[16,1,2]{2,1,0:T(1,128)S(1)} all-to-all(s32[16,1,2]{2,1,0:T(1,128)S(1)} %copy.36), channel_id=1, replica_groups=mesh['dp'=16,'tensor'=8] {'dp'}, dimensions={0} | all-to-all | bytes 256 | tf_op jit(solution)/shard_map/all_to_all | solution.py:92
  24.8 0.5 broadcast.174
  25.3 0.7 reduce.7
  26.0 0.1 reshape.181
  26.1 0.1 copy.37
  26.2 0.1 copy.38
  26.3 7.2 %gather_fusion = bf16[32,2,512,128]{3,2,1,0:T(8,128)(2,1)} fusion(bf16[16,2,512,128]{3,2,1,0:T(8,128)(2,1)} %param.11, s32[1024]{0:T(1024)S(1)} %pad_clamp_fusion.1), kind=kCustom, calls=%fused_computation | custom fusion | bytes 16777344 | tf_op jit(solution)/shard_map/jit(_take)/gather | solution.py:93
  33.5 7.5 %broadcast_select_fusion = bf16[16,2,2,512,128]{4,3,2,1,0:T(8,128)(2,1)} fusion(bf16[16,2,2,512,128]{4,3,2,1,0:T(8,128)(2,1)} %bitcast.140, pred[16,2]{1,0:T(8,128)(4,1)S(1)} %copy.38), kind=kLoop, calls=%fused_computation.13 | loop fusion | flops 4194304 | bytes 16777248 | tf_op jit(solution)/shard_map/jit(_take)/select_n | solution.py:93
  40.9 0.0 copy-start.4
  40.9 0.0 copy-start.6
  40.9 0.0 copy-start.3
  40.9 4.9 %all-to-all-start.1 = ((bf16[16,2,2,512,128]{4,3,2,1,0:T(8,128)(2,1)}), bf16[16,2,2,512,128]{4,3,2,1,0:T(8,128)(2,1)}, u32[]{:S(2)}, u32[]{:S(2)}) async-start(bf16[16,2,2,512,128]{4,3,2,1,0:T(8,128)(2,1)} %broadcast_select_fusion), calls=%async_computation.1 | async-start | bytes 16777216 | tf_op jit(solution)/shard_map/all_to_all | solution.py:96
  45.8 0.0 reduce-scatter.2.cloned.1.call-start
  45.9 0.0 copy-done.4
  45.9 0.0 copy-done.6
  45.9 0.1 select_reduce_fusion.1
  46.0 0.1 iota_compare_fusion.1
  46.1 0.0 copy-done
  46.1 0.0 copy-done.3
  46.1 4.1 %fusion.7 = (f32[16,8,64]{2,1,0:T(8,128)S(1)}, f32[16,64,64,8]{2,1,3,0:T(8,128)}) fusion(pred[64,64]{0,1:T(8,128)(4,1)S(1)} %iota_compare_fusion, bf16[16,2,64,128]{3,2,1,0:T(8,128)(2,1)S(1)} %copy-done.3, bf16[16,64,1024]{2,1,0:T(8,128)(2,1)S(1)} %copy-done), kind=kOutput, calls=%fused_computation.24 | convolution fusion | flops 135782400 | bytes 4497408 | tf_op jit(solution)/shard_map/bsngd,bund->bngsu/dot_general | solution.py:32
  50.2 116.6 %all-to-all-done.1 = bf16[16,2,2,512,128]{4,3,2,1,0:T(8,128)(2,1)} async-done(((bf16[16,2,2,512,128]{4,3,2,1,0:T(8,128)(2,1)}), bf16[16,2,2,512,128]{4,3,2,1,0:T(8,128)(2,1)}, u32[]{:S(2)}, u32[]{:S(2)}) %all-to-all-start.1) | async-done | bytes 8388640 | tf_op jit(solution)/shard_map/all_to_all | solution.py:96
  166.7 6.4 %gather_fusion.1 = bf16[16,2,512,128]{3,2,1,0:T(8,128)(2,1)} fusion(bf16[32,2,512,128]{3,2,1,0:T(8,128)(2,1)} %bitcast.9, s32[1024]{0:T(1024)S(1)} %pad_clamp_fusion), kind=kCustom, calls=%fused_computation.1 | custom fusion | bytes 8388672 | tf_op jit(solution)/shard_map/jit(_take)/gather | solution.py:98
  173.2 2.6 copy_select_fusion
  175.8 7.2 %bitcast_reduce_fusion = (f32[16,8,64]{2,1,0:T(8,128)S(1)}, f32[16,512,64,8]{1,2,3,0:T(8,128)}) fusion(pred[16,512]{1,0:T(8,128)(4,1)S(1)} %iota_compare_fusion.1, bf16[16,2,512,128]{3,2,0,1:T(8,128)(2,1)S(1)} %copy_select_fusion, bf16[16,64,1024]{2,1,0:T(8,128)(2,1)S(1)} %copy-done), kind=kOutput, calls=%fused_computation.4 | convolution fusion | flops 1086316544 | bytes 21012480 | tf_op jit(solution)/shard_map/bsngd,btnd->bngst/dot_general | solution.py:28
  183.0 0.0 copy-start.2
  183.0 8.4 %fusion.1 = f32[16,8,64]{2,1,0:T(8,128)S(1)} fusion(f32[16,512,64,8]{1,2,3,0:T(8,128)} %get-tuple-element.8, f32[16,8,64]{2,1,0:T(8,128)S(1)} %max.9, pred[16,512]{1,0:T(8,128)(4,1)S(1)} %iota_compare_fusion.1), kind=kLoop, calls=%fused_computation.9 | loop fusion | flops 16769024 | bytes 16850944 | tf_op jit(solution)/shard_map/reduce_sum | solution.py:47
  191.4 0.0 copy-done.2
  191.4 1.4 fusion.6
  192.8 10.3 %fusion.2 = f32[16,128,8,64]{1,3,2,0:T(8,128)S(1)} fusion(f32[16,512,64,8]{1,2,3,0:T(8,128)} %get-tuple-element.8, f32[16,8,64]{2,1,0:T(8,128)S(1)} %add.100, f32[16,8,64]{2,1,0:T(8,128)S(1)} %max.9, pred[16,512]{1,0:T(8,128)(4,1)S(1)} %iota_compare_fusion.1, bf16[16,2,512,128]{3,2,0,1:T(8,128)(2,1)S(1)} %copy_select_fusion), kind=kOutput, calls=%fused_computation.10 | convolution fusion | flops 1094713344 | bytes 23207936 | tf_op jit(solution)/shard_map/bngst,btnd->bsngd/dot_general | solution.py:52
  203.1 1.6 fusion.21
  204.7 1.8 copy.45
  206.5 25.8 %convolution_convert_fusion = bf16[1024,8192]{1,0:T(8,128)(2,1)} fusion(bf16[1024,8192]{1,0:T(8,128)(2,1)} %param.15, bf16[128,8,8,128]{3,2,1,0:T(8,128)(2,1)S(1)} %bitcast.141), kind=kOutput, calls=%fused_computation.8 | convolution fusion | flops 17188257792 | bytes 35651584 | tf_op jit(solution)/shard_map/dot_general | solution.py:101
  232.3 0.0 copy-start.5
  232.3 0.0 reduce-scatter.2.cloned.1.call-update
  232.4 0.7 copy-done.5
  233.0 93.5 %reduce-scatter.2.cloned.1.call-done = bf16[1024,1024]{1,0:T(8,128)(2,1)} async-done(((bf16[1024,8192]{1,0:T(8,128)(2,1)}), bf16[1024,1024]{1,0:T(8,128)(2,1)}) %reduce-scatter.2.cloned.1.call-update) | async-done | bytes 2097168 | tf_op jit(solution)/shard_map/reduce_scatter | solution.py:104
  326.5 0.0 copy-start.1
  326.5 3.1 multiply_reduce_fusion
  329.6 13.2 %psum.7 = f32[1024]{0:T(1024)S(1)} all-reduce(f32[1024]{0:T(1024)S(1)} %multiply_reduce_fusion), channel_id=1, replica_groups=mesh['dp'=16,'tensor'=8] {'tensor'}, use_global_device_ids=true, to_apply=%region_10.11 | all-reduce | flops 1024 | bytes 8192 | tf_op jit(solution)/shard_map/psum | solution.py:108
  342.8 4.3 %multiply_convert_fusion = bf16[1024,1024]{1,0:T(8,128)(2,1)} fusion(bf16[1024,1024]{1,0:T(8,128)(2,1)} %reduce-scatter.2.cloned.1.call-done, bf16[16,64,1024]{2,1,0:T(8,128)(2,1)} %param.16, f32[1024]{0:T(1024)S(1)} %convert_element_type.46, f32[1024]{0:T(1024)S(1)} %add_rsqrt_fusion), kind=kLoop, calls=%fused_computation.19 | loop fusion | flops 6291456 | bytes 6299648 | tf_op jit(solution)/shard_map/convert_element_type | solution.py:114
  347.1 0.0 copy-done.1
  (13 shorter events, 0.1 us)
Async XLA Ops:
  6.5 39.6 %copy-start = (bf16[16,64,1024]{2,1,0:T(8,128)(2,1)S(1)}, bf16[16,64,1024]{2,1,0:T(8,128)(2,1)}, u32[]{:S(2)}) copy-start(bf16[16,64,1024]{2,1,0:T(8,128)(2,1)} %param.9) | copy-start | bytes 6291460
  40.9 4.9 %copy-start.4 = (s32[16,1]{0,1:T(1,128)S(1)}, s32[16,1]{0,1:T(1,128)}, u32[]{:S(2)}) copy-start(s32[16,1]{0,1:T(1,128)} %param.12) | copy-start | bytes 196
  40.9 5.0 %copy-start.6 = (s32[8]{0:T(128)S(1)}, s32[8]{0:T(128)}, u32[]{:S(2)}) copy-start(s32[8]{0:T(128)} %param.14) | copy-start | bytes 100
  40.9 5.2 %copy-start.3 = (bf16[16,2,64,128]{3,2,1,0:T(8,128)(2,1)S(1)}, bf16[16,2,64,128]{3,2,1,0:T(8,128)(2,1)}, u32[]{:S(2)}) copy-start(bf16[16,2,64,128]{3,2,1,0:T(8,128)(2,1)} %param.10) | copy-start | bytes 1572868
  40.9 125.8 %all-to-all-start.1 = ((bf16[16,2,2,512,128]{4,3,2,1,0:T(8,128)(2,1)}), bf16[16,2,2,512,128]{4,3,2,1,0:T(8,128)(2,1)}, u32[]{:S(2)}, u32[]{:S(2)}) async-start(bf16[16,2,2,512,128]{4,3,2,1,0:T(8,128)(2,1)} %broadcast_select_fusion), calls=%async_computation.1 | async-start | bytes 16777216 | tf_op jit(solution)/shard_map/all_to_all | solution.py:96
  45.8 280.7 %reduce-scatter.2.cloned.1.call-start = ((), (), s32[]{:S(2)}) async-start(), calls=%async_computation.3 | async-start | bytes 18874368 | tf_op jit(solution)/shard_map/reduce_scatter | solution.py:104
  183.0 8.4 %copy-start.2 = (f32[16,64,64,8]{2,1,3,0:T(8,128)S(1)}, f32[16,64,64,8]{2,1,3,0:T(8,128)}, u32[]{:S(2)}) copy-start(f32[16,64,64,8]{2,1,3,0:T(8,128)} %get-tuple-element.10) | copy-start | bytes 6291460
  232.3 0.7 copy-start.5
  326.5 20.6 %copy-start.1 = (bf16[16,64,1024]{2,1,0:T(8,128)(2,1)S(1)}, bf16[16,64,1024]{2,1,0:T(8,128)(2,1)}, u32[]{:S(2)}) copy-start(bf16[16,64,1024]{2,1,0:T(8,128)(2,1)} %param.9) | copy-start | bytes 6291460
Sparse Core Ops, SparseCore 0:
  232.5 93.9 reduce-scatter.1
where the time goes:
time: 355 us; the launch traced here: 354 us
  waiting for transfers between devices  210 us (59%)
  matrix products  48.9 us (14%)
  other arithmetic  31.3 us (9%)
  blocking collectives  26.9 us (8%)
  local copies, waits for them, and re-layouts  18.2 us (5%)
  between operations  13.6 us (4%)
  starting transfers between devices  4.91 us (1%)
    all_to_all x1, waiting for transfers between devices, on_device(): lax.all_to_all(outgoing, 'dp', split_axis=0, concat_axis=0, tiled=True)  117 us
    reduce_scatter x1, waiting for transfers between devices, on_device(): lax.psum_scatter(partial_terms.astype(jnp.bfloat16), 'tensor', scatter_di...  93.5 us
    dot_general x1, matrix products, on_device(): jnp.dot(mixed_heads.reshape(row_total, width_query), out_weight, preferre...  25.8 us
    all_to_all x1, blocking collectives, on_device(): lax.all_to_all(request, 'dp', split_axis=0, concat_axis=0, tiled=True)  13.8 us
    psum x1, blocking collectives, on_device(): squares = lax.psum(jnp.sum(attended * attended, axis=1), 'tensor')  13.2 us
    dot_general x1, matrix products, attend(): jnp.einsum('bngst,btnd->bsngd', cache_weights, cached_values, preferred_e...  10.3 us
    reduce_sum x1, other arithmetic, attend(): jnp.sum(cache_probs, axis=-1, keepdims=True)  8.35 us
    select_n x2, other arithmetic, on_device(): jnp.take(kv_cache, asked_slots.reshape(-1), axis=0)  7.46 us
  transfers between devices with their start and end apart: 2, of which 2 were waited for; matrix products, arithmetic and copies ran while one was open for 1% of the time, Pallas kernels for 0%

commit v1 on v0

v1 whole, which is shorter than its diff:
```python
import functools
import math

import jax
import jax.numpy as jnp
from jax import lax
from jax.experimental import pallas as pl
from jax.experimental.pallas import tpu as pltpu
from jax.sharding import PartitionSpec as P

MESH = pl.DeviceIdType.MESH
HEAD = 128
BLK = 16
LANES = 128
EPS = 1e-06
F32 = jnp.float32
BF16 = jnp.bfloat16
STRIDE = 7


class Plan:
    def __init__(self, n, tensor, beams, step, ctx, width, problems, model):
        self.n, self.tensor, self.zs = n, tensor, tensor // 2
        self.beams, self.step, self.ctx, self.width = beams, step, ctx, width
        self.problems, self.ranks, self.model = problems, beams // problems, model
        self.side = math.isqrt(n)
        total = problems * ctx * 5 // 8
        rest = total - ctx
        before = [
            (rest * j // (problems - 1) + (BLK - 1) * j) // BLK for j in range(problems)
        ]
        before.append(ctx // BLK + before[problems - 1])
        ends = [1, 3, 5, 7, 8] if problems == 8 else list(range(1, problems + 1))
        self.chunks, self.turns = [], []
        low, turn = 0, 0
        for end in ends:
            last = -(-before[end] // n)
            self.chunks.append((low, end))
            self.turns.append((turn, last))
            low, turn = end, last
        self.slots = turn * n
        self.blocks = ctx // BLK
        self.most = []
        for j in range(problems):
            bound = rest // (problems - 1 - j) if j < problems - 1 else ctx
            self.most.append(min(ctx, -(-bound // LANES) * LANES))
        self.rows = max(
            [self.slots * BLK] + [before[j] * BLK + self.most[j] for j in range(problems)]
        )
        self.rows = -(-self.rows // BLK) * BLK
        self.row_most = max(e - s for s, e in self.chunks) * self.ranks * step
        self.turn_most = max(e - s for s, e in self.turns)


def kernel(plan, names, *refs):
    r = dict(zip(names, refs))
    n, zs, tensor = plan.n, plan.zs, plan.tensor
    ranks, problems, step, width = plan.ranks, plan.problems, plan.step, plan.width
    heads = width // HEAD
    side = plan.side
    count = len(plan.chunks)
    slots = plan.slots
    me = lax.axis_index("dp")
    mine = lax.axis_index("tensor")
    my_y, my_x = me // side, me % side
    my_z, my_core = mine // 2, mine % 2
    tab, reqs = r["tab"], r["reqs"]
    at_order, at_off, at_len, at_rank = (2 * slots + problems * i for i in range(4))

    def plane_peer(index):
        hop = (index * STRIDE) % n
        there = ((my_y + hop // side) % side) * side + (my_x + hop % side) % side
        return hop, there

    def tensor_peer(hop):
        return (mine + hop) % tensor

    def chip_at(hop):
        return (my_z + hop) % zs

    loads = {}
    for i, name in enumerate(("kv", "q", "fresh", "wt", "res")):
        loads[name] = pltpu.make_async_copy(r[name + "_h"], r[name], r["load_sem"].at[i])
        loads[name].start()

    barrier = pltpu.get_barrier_semaphore()

    @pl.loop(1, n)
    def _(index):
        hop, there = plane_peer(index)
        pl.semaphore_signal(barrier, inc=1, device_id=(there, mine), device_id_type=MESH)

    @pl.loop(1, tensor)
    def _(hop):
        pl.semaphore_signal(
            barrier, inc=1, device_id=(me, tensor_peer(hop)), device_id_type=MESH
        )

    loads["kv"].wait()
    pl.semaphore_wait(barrier, n - 1 + tensor - 1)

    def request_copy(index):
        hop, there = plane_peer(index)
        return pltpu.make_async_remote_copy(
            src_ref=r["req"],
            dst_ref=r["reqv"].at[me],
            send_sem=r["rq_s"].at[hop],
            recv_sem=r["rq_r"].at[hop],
            device_id=(there, mine),
            device_id_type=MESH,
        )

    @pl.loop(1, n)
    def _(index):
        request_copy(index).start()

    r["reqv"][me] = r["req"][...]

    def spread_copy(c, index):
        hop, there = plane_peer(index)
        lo, hi = plan.turns[c]
        return pltpu.make_async_remote_copy(
            src_ref=r["send1"].at[c % 2, there, pl.ds(0, ranks), pl.ds(0, hi - lo)],
            dst_ref=r[f"stash{c}"].at[pl.ds(me * ranks, ranks)],
            send_sem=r["p1_s"].at[c, hop],
            recv_sem=r["p1_r"].at[c, hop],
            device_id=(there, mine),
            device_id_type=MESH,
        )

    def fetch_copy(c, index):
        hop, there = plane_peer(index)
        lo, hi = plan.turns[c]
        return pltpu.make_async_remote_copy(
            src_ref=r["send2"].at[c % 2, there, pl.ds(0, ranks), pl.ds(0, hi - lo)],
            dst_ref=r[f"got{c}"].at[me],
            send_sem=r["p2_s"].at[c, hop],
            recv_sem=r["p2_r"].at[c, hop],
            device_id=(there, mine),
            device_id_type=MESH,
        )

    def each_peer(make, c, what):
        @pl.loop(1, n)
        def _(index):
            getattr(make(c, index), what)()

    def spread(c):
        lo, hi = plan.turns[c]
        if c >= 2:
            each_peer(spread_copy, c - 2, "wait_send")

        @pl.loop(0, n)
        def _(k):
            for i in range(lo, hi):
                problem = tab[i * n + k]
                block = tab[slots + i * n + k]
                for rank in range(ranks):
                    r["send1"][c % 2, k, rank, i - lo] = r["kv"][
                        rank * problems + problem, :, block
                    ]

        each_peer(spread_copy, c, "start")
        for rank in range(ranks):
            r[f"stash{c}"][me * ranks + rank] = r["send1"][c % 2, me, rank, : hi - lo]

    def fetch(c):
        lo, hi = plan.turns[c]
        each_peer(spread_copy, c, "wait_recv")
        if c >= 2:
            each_peer(fetch_copy, c - 2, "wait_send")

        @pl.loop(0, n)
        def _(child):
            for i in range(lo, hi):
                problem = tab[i * n + me]
                for slot in range(ranks):
                    parent = reqs[child, 0, slot * problems + problem]
                    r["send2"][c % 2, child, slot, i - lo] = r[f"stash{c}"][parent, i - lo]

        each_peer(fetch_copy, c, "start")
        r[f"got{c}"][me] = r["send2"][c % 2, me, :, : hi - lo]

    def unpack(c):
        lo, hi = plan.turns[c]
        each_peer(fetch_copy, c, "wait_recv")

        @pl.loop(0, n)
        def _(k):
            for i in range(lo, hi):
                for slot in range(ranks):
                    for part, name in enumerate(("kbuf", "vbuf")):
                        r[name][slot, i * n + k] = r[f"got{c}"][k, slot, i - lo, part]

    group = min(4, heads)
    factor = math.log2(math.e) / math.sqrt(HEAD)
    nt = (((1,), (1,)), ((), ()))

    def attend(c):
        first, last = plan.chunks[c]
        span = plan.most[last - 1]

        @pl.loop(0, (last - first) * ranks)
        def _(e):
            j = first + e // ranks
            slot = e % ranks
            beam = slot * problems + tab[at_order + j]
            start = tab[at_off + j]
            live = tab[at_len + j]
            keys, values = (
                jnp.concatenate([r[name][slot, start + i] for i in range(span // BLK)], axis=0)
                for name in ("kbuf", "vbuf")
            )
            new_keys, new_values = r["fresh"][beam, 0], r["fresh"][beam, 1]
            values = jnp.concatenate([values, jnp.ones_like(values)], axis=1)
            new_values = jnp.concatenate([new_values, jnp.ones_like(new_values)], axis=1)
            query = r["q"][beam]
            place = pl.multiple_of(e * step, step)
            for g in range(0, heads, group):
                part = jnp.concatenate(
                    [query[:, (g + h) * HEAD : (g + h + 1) * HEAD] for h in range(group)], axis=0
                )
                old = lax.dot_general(part, keys, nt, preferred_element_type=F32)
                new = lax.dot_general(part, new_keys, nt, preferred_element_type=F32)
                where = lax.broadcasted_iota(jnp.int32, old.shape, 1)
                old = jnp.where(where < live, old, -1e30)
                token = lax.broadcasted_iota(jnp.int32, new.shape, 0) % step
                other = lax.broadcasted_iota(jnp.int32, new.shape, 1)
                new = jnp.where(other <= token, new, -1e30)
                top = jnp.maximum(
                    jnp.max(old, axis=1, keepdims=True), jnp.max(new, axis=1, keepdims=True)
                )
                old = jnp.exp2((old - top) * factor).astype(BF16)
                new = jnp.exp2((new - top) * factor).astype(BF16)
                out = jnp.dot(old, values, preferred_element_type=F32)
                out = out + jnp.dot(new, new_values, preferred_element_type=F32)
                out = (out[:, :HEAD] / out[:, HEAD:]).astype(BF16)
                for h in range(group):
                    r["mixed"][pl.ds(place, step), (g + h) * HEAD : (g + h + 1) * HEAD] = out[
                        h * step : (h + 1) * step
                    ]

    def rows_of(c):
        first, last = plan.chunks[c]
        return (last - first) * ranks * step

    tile = min(256, width)

    def project(c, block, target):
        rows = rows_of(c)

        @pl.loop(0, width // tile)
        def _(k):
            here = pl.multiple_of(k * tile, tile)
            column = pl.multiple_of(block * width + here, tile)
            value = jnp.dot(
                r["mixed"][:rows, :], r["wt"][:, pl.ds(column, tile)], preferred_element_type=F32
            )
            target[:rows, pl.ds(here, tile)] = value.astype(BF16)

    pending = {}

    def core_copy(c, hop):
        rows = rows_of(c)
        return pltpu.make_async_remote_copy(
            src_ref=r["csend"].at[hop, pl.ds(0, rows)],
            dst_ref=r["crecv"].at[c % 2, hop, pl.ds(0, rows)],
            send_sem=r["c_s"].at[hop],
            recv_sem=r["c_r"].at[c, hop],
            device_id=(me, my_z * 2 + 1 - my_core),
            device_id_type=MESH,
        )

    def block_for(c, hop):
        if c >= 1:
            pending["core", c - 1, hop].wait_send()
        project(c, chip_at(hop) * 2 + 1 - my_core, r["csend"].at[hop])
        pending["core", c, hop] = core_copy(c, hop)
        pending["core", c, hop].start()
        project(c, chip_at(hop) * 2 + my_core, r["own"].at[c % 2, hop])

    def z_copy(c, kind, way):
        rows = rows_of(c)
        hop = (1, zs - 1)[way]
        if kind == "t":
            src = r["tsend"].at[pl.ds(way * (rows // 2), rows // 2)]
            dst = r[f"trecv{c}"].at[way]
        else:
            src = r["dsend"].at[way, pl.ds(0, rows)]
            dst = r[f"drecv{c}"].at[way]
        return pltpu.make_async_remote_copy(
            src_ref=src,
            dst_ref=dst,
            send_sem=r[kind + "_s"].at[way],
            recv_sem=r[kind + "_r"].at[c, way],
            device_id=(me, chip_at(hop) * 2 + my_core),
            device_id_type=MESH,
        )

    opposite = zs // 2
    piece = 32

    def send_far(c):
        rows = rows_of(c)
        pending["core", c, opposite].wait_recv()
        if c >= 1:
            for way in range(2):
                pending["t", c - 1, way].wait_send()

        @pl.loop(0, rows // piece)
        def _(i):
            at = pl.ds(pl.multiple_of(i * piece, piece), piece)
            value = r["own"][c % 2, opposite, at, :].astype(F32)
            value = value + r["crecv"][c % 2, opposite, at, :].astype(F32)
            r["tsend"][at, :] = value.astype(BF16)

        for way in range(2):
            pending["t", c, way] = z_copy(c, "t", way)
            pending["t", c, way].start()

    def send_near(c):
        rows = rows_of(c)
        half = rows // 2
        for way in range(2):
            hop = (1, zs - 1)[way]
            pending["core", c, hop].wait_recv()
            pending["t", c, way].wait_recv()
            if c >= 1:
                pending["d", c - 1, way].wait_send()

            @pl.loop(0, half // piece)
            def _(i):
                at = pl.ds(pl.multiple_of((1 - way) * half + i * piece, piece), piece)
                value = r["own"][c % 2, hop, at, :].astype(F32)
                value = value + r["crecv"][c % 2, hop, at, :].astype(F32)
                r["dsend"][way, at, :] = value.astype(BF16)

            @pl.loop(0, half // piece)
            def _(i):
                start = pl.multiple_of(i * piece, piece)
                at = pl.ds(pl.multiple_of(way * half + i * piece, piece), piece)
                value = r["own"][c % 2, hop, at, :].astype(F32)
                value = value + r["crecv"][c % 2, hop, at, :].astype(F32)
                value = value + r[f"trecv{c}"][way, pl.ds(start, piece), :].astype(F32)
                r["dsend"][way, at, :] = value.astype(BF16)

            pending["d", c, way] = z_copy(c, "d", way)
            pending["d", c, way].start()

    def square_copy(c, hop):
        return pltpu.make_async_remote_copy(
            src_ref=r[f"sq{c}"],
            dst_ref=r[f"sqr{c}"].at[mine],
            send_sem=r["s_s"].at[c, hop],
            recv_sem=r["s_r"].at[c, hop],
            device_id=(me, tensor_peer(hop)),
            device_id_type=MESH,
        )

    def finish(c):
        first, last = plan.chunks[c]
        pending["core", c, 0].wait_recv()
        for way in range(2):
            pending["d", c, way].wait_recv()

        @pl.loop(0, (last - first) * ranks)
        def _(e):
            j = first + e // ranks
            slot = e % ranks
            beam = slot * problems + tab[at_order + j]
            for low in range(0, step, 32):
                at = pl.ds(pl.multiple_of(e * step + low, 32), 32)
                value = r["own"][c % 2, 0, at, :].astype(F32)
                value = value + r["crecv"][c % 2, 0, at, :].astype(F32)
                value = value + r[f"drecv{c}"][0, at, :].astype(F32)
                value = value + r[f"drecv{c}"][1, at, :].astype(F32)
                value = value + r["res"][beam, low : low + 32, :].astype(F32)
                place = pl.ds(pl.multiple_of(slot * step + low, 32), 32)
                r["att"][j, place, :] = value
                value = value * value
                total = value[:, :LANES]
                for k in range(LANES, width, LANES):
                    total = total + value[:, k : k + LANES]
                r["sums"][e // ranks, place, :] = total

        for k in range(last - first):
            line = jnp.sum(r["sums"][k].T, axis=0, keepdims=True)
            r[f"sq{c}"][k] = jnp.broadcast_to(line, (8, line.shape[1]))
        r[f"sqr{c}"][mine] = r[f"sq{c}"][...]

        @pl.loop(1, tensor)
        def _(hop):
            square_copy(c, hop).start()

        if c + 2 < count:
            pl.semaphore_signal(
                r["credit"],
                inc=1,
                device_id=(me, my_z * 2 + 1 - my_core),
                device_id_type=MESH,
            )

    def project_all(c):
        if c >= 2:
            finish(c - 2)
            pl.semaphore_wait(r["credit"], 1)
        hops = [opposite, 1, zs - 1, 0]
        block_for(c, hops[0])
        block_for(c, hops[1])
        send_far(c)
        block_for(c, hops[2])
        block_for(c, hops[3])

    spread(0)
    if count > 1:
        spread(1)

    @pl.loop(1, n)
    def _(index):
        request_copy(index).wait_recv()

    table = pltpu.make_async_copy(r["reqv"], reqs, r["table_sem"])
    table.start()

    @pl.loop(0, plan.rows // BLK)
    def _(i):
        for name in ("kbuf", "vbuf"):
            for slot in range(ranks):
                r[name][slot, i] = jnp.zeros((BLK, HEAD), BF16)

    table.wait()
    fetch(0)
    if count > 2:
        spread(2)
    for name in ("q", "fresh", "wt", "res"):
        loads[name].wait()

    for c in range(count):
        if c + 1 < count:
            fetch(c + 1)
        if c + 3 < count:
            spread(c + 3)
        unpack(c)
        attend(c)
        if c >= 1:
            send_near(c - 1)
        project_all(c)
    send_near(count - 1)
    if count > 1:
        finish(count - 2)
    finish(count - 1)

    for c, (first, last) in enumerate(plan.chunks):

        @pl.loop(1, tensor)
        def _(hop):
            square_copy(c, hop).wait_recv()

        for k in range(last - first):
            line = r[f"sqr{c}"][0, k]
            for t in range(1, tensor):
                line = line + r[f"sqr{c}"][t, k]
            line = lax.rsqrt(line / plan.model + EPS)
            wide = jnp.broadcast_to(line[0:1, :], (LANES, line.shape[1]))
            r["scale"][first + k] = wide.T

    def out_copy(problem, slot):
        beam = slot * problems + problem
        return pltpu.make_async_copy(
            r["res"].at[beam], r["out_h"].at[beam], r["out_sem"].at[beam]
        )

    @pl.loop(0, problems)
    def _(problem):
        j = tab[at_rank + problem]
        for slot in range(ranks):
            for low in range(0, step, 32):
                at = slice(slot * step + low, slot * step + low + 32)
                scale = r["scale"][j, at, :]
                for k in range(0, width, LANES):
                    value = r["att"][j, at, k : k + LANES] * scale
                    value = value * r["gain"][:, k : k + LANES].astype(F32)
                    r["res"][slot * problems + problem, low : low + 32, k : k + LANES] = (
                        value.astype(BF16)
                    )
            out_copy(problem, slot).start()

    @pl.loop(0, problems)
    def _(problem):
        for slot in range(ranks):
            out_copy(problem, slot).wait()

    @pl.loop(1, n)
    def _(index):
        request_copy(index).wait_send()

    for c in range(max(0, count - 2), count):
        each_peer(spread_copy, c, "wait_send")
        each_peer(fetch_copy, c, "wait_send")
    for hop in range(zs):
        pending["core", count - 1, hop].wait_send()
    for way in range(2):
        pending["t", count - 1, way].wait_send()
        pending["d", count - 1, way].wait_send()
    for c in range(count):

        @pl.loop(1, tensor)
        def _(hop):
            square_copy(c, hop).wait_send()


def tables(plan, cache_length, parent_device, parent_rank):
    problems = plan.problems
    lengths = cache_length.astype(jnp.int32)
    ids = jnp.arange(problems, dtype=jnp.int32)
    below = (lengths[None, :] < lengths[:, None]) | (
        (lengths[None, :] == lengths[:, None]) & (ids[None, :] < ids[:, None])
    )
    rank = jnp.sum(below.astype(jnp.int32), axis=1)
    chosen = (rank[None, :] == ids[:, None]).astype(jnp.int32)
    order = jnp.sum(chosen * ids[None, :], axis=1)
    live = jnp.sum(chosen * lengths[None, :], axis=1)
    used = (lengths + BLK - 1) // BLK
    start = jnp.sum(jnp.where(rank[None, :] < ids[:, None], used[None, :], 0), axis=1)
    slot = jnp.arange(plan.slots, dtype=jnp.int32)
    turn = jnp.sum((start[None, 1:] <= slot[:, None]).astype(jnp.int32), axis=1)
    mine = (turn[:, None] == ids[None, :]).astype(jnp.int32)
    problem = jnp.sum(mine * order[None, :], axis=1)
    block = jnp.clip(slot - jnp.sum(mine * start[None, :], axis=1), 0, plan.blocks - 1)
    tab = jnp.concatenate([problem, block, order, start, live, rank])
    wanted = parent_device[:, 0] * plan.ranks + parent_rank
    req = jnp.zeros((8, LANES), jnp.int32).at[0, : plan.beams].set(wanted)
    return tab, req


def on_device(
    queries, fresh_kv, kv_cache, parent_device, parent_rank, cache_length, out_weight, residual,
    norm_gain,
):
    n, tensor = lax.axis_size("dp"), lax.axis_size("tensor")
    beams, step, width = queries.shape
    ctx = kv_cache.shape[2]
    plan = Plan(n, tensor, beams, step, ctx, width, cache_length.shape[0], width * tensor)
    tab, req = tables(plan, cache_length, parent_device, parent_rank)
    count, ranks, most = len(plan.chunks), plan.ranks, plan.row_most
    blocks = kv_cache.reshape(beams, 2, plan.blocks, BLK, HEAD)

    smem = pl.BlockSpec(memory_space=pltpu.SMEM)
    vmem = pl.BlockSpec(memory_space=pltpu.VMEM)
    hbm = pl.BlockSpec(memory_space=pl.ANY)
    inputs = [
        ("tab", tab, smem),
        ("req", req, vmem),
        ("gain", norm_gain.reshape(1, width), vmem),
        ("q_h", queries, hbm),
        ("fresh_h", fresh_kv, hbm),
        ("kv_h", blocks, hbm),
        ("wt_h", out_weight, hbm),
        ("res_h", residual, hbm),
    ]
    dma = lambda *shape: pltpu.SemaphoreType.DMA(shape)
    scratch = [
        ("q", pltpu.VMEM(queries.shape, BF16)),
        ("fresh", pltpu.VMEM(fresh_kv.shape, BF16)),
        ("kv", pltpu.VMEM(blocks.shape, BF16)),
        ("wt", pltpu.VMEM(out_weight.shape, BF16)),
        ("res", pltpu.VMEM(residual.shape, BF16)),
        ("kbuf", pltpu.VMEM((ranks, plan.rows // BLK, BLK, HEAD), BF16)),
        ("vbuf", pltpu.VMEM((ranks, plan.rows // BLK, BLK, HEAD), BF16)),
        ("send1", pltpu.VMEM((2, n, ranks, plan.turn_most, 2, BLK, HEAD), BF16)),
        ("send2", pltpu.VMEM((2, n, ranks, plan.turn_most, 2, BLK, HEAD), BF16)),
        ("reqv", pltpu.VMEM((n, 8, LANES), jnp.int32)),
        ("reqs", pltpu.SMEM((n, 8, LANES), jnp.int32)),
        ("mixed", pltpu.VMEM((most, width), BF16)),
        ("own", pltpu.VMEM((2, plan.zs, most, width), BF16)),
        ("csend", pltpu.VMEM((plan.zs, most, width), BF16)),
        ("crecv", pltpu.VMEM((2, plan.zs, most, width), BF16)),
        ("tsend", pltpu.VMEM((most, width), BF16)),
        ("dsend", pltpu.VMEM((2, most, width), BF16)),
        ("att", pltpu.VMEM((plan.problems, ranks * step, width), F32)),
        ("sums", pltpu.VMEM((most // (ranks * step), ranks * step, LANES), F32)),
        ("scale", pltpu.VMEM((plan.problems, ranks * step, LANES), F32)),
        ("load_sem", dma(5)),
        ("table_sem", pltpu.SemaphoreType.DMA),
        ("rq_s", dma(n)),
        ("rq_r", dma(n)),
        ("p1_s", dma(count, n)),
        ("p1_r", dma(count, n)),
        ("p2_s", dma(count, n)),
        ("p2_r", dma(count, n)),
        ("c_s", dma(plan.zs)),
        ("c_r", dma(count, plan.zs)),
        ("t_s", dma(2)),
        ("t_r", dma(count, 2)),
        ("d_s", dma(2)),
        ("d_r", dma(count, 2)),
        ("s_s", dma(count, tensor)),
        ("s_r", dma(count, tensor)),
        ("out_sem", dma(beams)),
        ("credit", pltpu.SemaphoreType.REGULAR),
    ]
    for c in range(count):
        (first, last), (lo, hi) = plan.chunks[c], plan.turns[c]
        rows = (last - first) * ranks * step
        scratch += [
            (f"stash{c}", pltpu.VMEM((n * ranks, hi - lo, 2, BLK, HEAD), BF16)),
            (f"got{c}", pltpu.VMEM((n, ranks, hi - lo, 2, BLK, HEAD), BF16)),
            (f"trecv{c}", pltpu.VMEM((2, rows // 2, width), BF16)),
            (f"drecv{c}", pltpu.VMEM((2, rows, width), BF16)),
            (f"sq{c}", pltpu.VMEM((last - first, 8, ranks * step), F32)),
            (f"sqr{c}", pltpu.VMEM((tensor, last - first, 8, ranks * step), F32)),
        ]
    names = [i[0] for i in inputs] + ["out_h"] + [s[0] for s in scratch]
    rows = beams * step
    return pl.pallas_call(
        functools.partial(kernel, plan, names),
        out_shape=jax.ShapeDtypeStruct(residual.shape, BF16),
        in_specs=[i[2] for i in inputs],
        out_specs=hbm,
        scratch_shapes=[s[1] for s in scratch],
        compiler_params=pltpu.CompilerParams(
            collective_id=0, has_side_effects=True, vmem_limit_bytes=64 * 1024 * 1024 - 4096
        ),
        cost_estimate=pl.CostEstimate(
            flops=2 * rows * width * width * tensor + 4 * rows * width * (ctx + step),
            bytes_accessed=30 * 1024 * 1024,
            transcendentals=rows * (width // HEAD) * (ctx + step),
        ),
        name="step_scoring",
    )(*[i[1] for i in inputs])


def solution(mesh):
    placed = (
        P("dp", None, "tensor"),
        P("dp", None, None, "tensor"),
        P("dp", None, None, "tensor"),
        P("dp", None),
        P("dp"),
        P(),
        P("tensor", None),
        P("dp", None, "tensor"),
        P("tensor"),
    )
    return jax.shard_map(
        on_device, mesh=mesh, in_specs=placed, out_specs=P("dp", None, "tensor"), check_vma=False
    )
```

time: 355 us -> 146 us (0.41)
  waiting for transfers between devices: 210 us -> 0 us
  Pallas kernels: 0 us -> 137 us
  matrix products: 48.9 us -> 0 us
  other arithmetic: 31.3 us -> 3.24 us
  blocking collectives: 26.9 us -> 0 us
  between operations: 13.6 us -> 0.03 us
  local copies, waits for them, and re-layouts: 18.2 us -> 5.75 us
  starting transfers between devices: 4.91 us -> 0 us
    pallas_call x0 -> x1, Pallas kernels: none -> 137 us  [on_device(): pl.pallas_call(functools.partial(kernel, plan, names), out_shape=jax.Shap...]
    all_to_all x1 -> x0, waiting for transfers between devices: 117 us -> none  [on_device(): lax.all_to_all(outgoing, 'dp', split_axis=0, concat_axis=0, tiled=True)]
    reduce_scatter x1 -> x0, waiting for transfers between devices: 93.5 us -> none  [on_device(): lax.psum_scatter(partial_terms.astype(jnp.bfloat16), 'tensor', scatter_di...]
    dot_general x5 -> x0, matrix products: 48.9 us -> none  [the longest x1 25.8 us: on_device(): jnp.dot(mixed_heads.reshape(row_total, width_query), out_weight, preferre...]
    all_to_all x1 -> x0, blocking collectives: 13.8 us -> none  [on_device(): lax.all_to_all(request, 'dp', split_axis=0, concat_axis=0, tiled=True)]
    gather x2 -> x0, local copies, waits for them, and re-layouts: 13.6 us -> none  [the longest x1 7.2 us: on_device(): jnp.take(kv_cache, asked_slots.reshape(-1), axis=0)]
    psum x1 -> x0, blocking collectives: 13.2 us -> none  [on_device(): squares = lax.psum(jnp.sum(attended * attended, axis=1), 'tensor')]
    reduce_sum x5 -> x4, other arithmetic: 13.8 us -> 1.89 us  [the longest x1 0.91 us: tables(): rank = jnp.sum(below.astype(jnp.int32), axis=1)]
  transfers between devices with their start and end apart: 2 -> 0, of which waited for: 2 -> 0; matrix products, arithmetic and copies ran while one was open for 1% -> 0% of each run, Pallas kernels for 0% -> 0%
where the time goes in v1:
time: 146 us
  Pallas kernels  137 us (94%)
  local copies, waits for them, and re-layouts  5.75 us (4%)
  other arithmetic  3.24 us (2%)
    pallas_call x1, Pallas kernels, on_device(): pl.pallas_call(functools.partial(kernel, plan, names), out_shape=jax.Shap...  137 us
    unnamed x1, local copies, waits for them, and re-layouts  3.14 us

profile of v1, /device:TPU:1, one launch (start us, length us, event | category | flops | bytes accessed | tf_op | source)
XLA Modules:
  0.0 146.1 jit_solution(10236489281459657619)
XLA Ops:
  0.0 0.9 convert_reduce_fusion.1
  0.9 0.7 fusion.2
  1.6 0.7 and_select_fusion
  2.3 0.8 select_reduce_fusion.2
  3.1 0.1 slice.19
  3.1 0.1 convert_reduce_fusion
  3.2 0.1 select_reduce_fusion
  3.3 0.7 concatenate.5.refs_0_
  4.0 0.6 scatter.4.refs_1_
  4.6 1.3 reshape.47.refs_2_
  5.9 137.1 %step_scoring.1 = bf16[16,64,1024]{2,1,0:T(8,128)(2,1)} custom-call(s32[384]{0:T(512)} %concatenate.5.refs_0_, s32[8,128]{1,0:T(8,128)} %scatter.4.refs_1_, bf16[1,1024]{1,0:T(2,128)(2,1)} %reshape.47.refs_2_, bf16[16,64,1024]{2,1,0:T(8,128)(2,1)} %refs_3_.1, bf16[16,2,64,128]{3,2,1,0:T(8,128)(2,1)} %refs_4_.1, bf16[16,2,32,16,128]{4,3,2,1,0:T(8,128)(2,1)} %bitcast.7, ...), custom_call_target="tpu_custom_call" | custom-call | flops 19595788288 | bytes 31457280 | tf_op jit(solution)/shard_map/step_scoring/pallas_call | solution.py:615
  143.0 3.1 %copy.11 = bf16[16,64,1024]{2,1,0:T(8,128)(2,1)} copy(bf16[16,64,1024]{2,1,0:T(8,128)(2,1)} %step_scoring.1) | data formatting | bytes 4194304
  (1 shorter events, 0.0 us)

commit v2 on v1

--- a/solution.py
+++ b/solution.py
@@ -78,11 +78,6 @@
     def chip_at(hop):
         return (my_z + hop) % zs
 
-    loads = {}
-    for i, name in enumerate(("kv", "q", "fresh", "wt", "res")):
-        loads[name] = pltpu.make_async_copy(r[name + "_h"], r[name], r["load_sem"].at[i])
-        loads[name].start()
-
     barrier = pltpu.get_barrier_semaphore()
 
     @pl.loop(1, n)
@@ -96,7 +91,50 @@
             barrier, inc=1, device_id=(me, tensor_peer(hop)), device_id_type=MESH
         )
 
-    loads["kv"].wait()
+    loads = {}
+    for i, name in enumerate(("kv", "q", "fresh", "wt", "res")):
+        loads[name] = pltpu.make_async_copy(r[name + "_h"], r[name], r["load_sem"].at[i])
+    loads["kv"].start()
+
+    lengths = [r["length"][p] for p in range(problems)]
+    rank_of = []
+    for p in range(problems):
+        found = jnp.int32(0)
+        for o in range(problems):
+            if o != p:
+                ahead = lengths[o] <= lengths[p] if o < p else lengths[o] < lengths[p]
+                found = found + jnp.where(ahead, 1, 0)
+        rank_of.append(found)
+        tab[at_rank + p] = found
+    starts = []
+    for j in range(problems):
+        which, long, start = jnp.int32(0), jnp.int32(0), jnp.int32(0)
+        for p in range(problems):
+            hit = rank_of[p] == j
+            which = which + jnp.where(hit, p, 0)
+            long = long + jnp.where(hit, lengths[p], 0)
+            used = lax.div(lengths[p] + (BLK - 1), jnp.int32(BLK))
+            start = start + jnp.where(rank_of[p] < j, used, 0)
+        tab[at_order + j], tab[at_len + j], tab[at_off + j] = which, long, start
+        starts.append(start)
+
+    def place(lo, hi):
+        @pl.loop(lo * n, hi * n)
+        def _(slot):
+            turn = jnp.int32(0)
+            for j in range(1, problems):
+                turn = turn + jnp.where(starts[j] <= slot, 1, 0)
+            tab[slot] = tab[at_order + turn]
+            block = slot - tab[at_off + turn]
+            tab[slots + slot] = jnp.minimum(jnp.maximum(block, 0), plan.blocks - 1)
+
+    lane = lax.broadcasted_iota(jnp.int32, (8, LANES), 1)
+    wanted = jnp.zeros((8, LANES), jnp.int32)
+    for b in range(plan.beams):
+        value = r["device"][b] * ranks + r["rank"][b]
+        wanted = jnp.where(lane == b, value, wanted)
+    r["req"][...] = wanted
+
     pl.semaphore_wait(barrier, n - 1 + tensor - 1)
 
     def request_copy(index):
@@ -147,10 +185,11 @@
 
     def spread(c):
         lo, hi = plan.turns[c]
+        place(lo, hi)
         if c >= 2:
             each_peer(spread_copy, c - 2, "wait_send")
 
-        @pl.loop(0, n)
+        @pl.loop(0, n, unroll=2)
         def _(k):
             for i in range(lo, hi):
                 problem = tab[i * n + k]
@@ -170,7 +209,7 @@
         if c >= 2:
             each_peer(fetch_copy, c - 2, "wait_send")
 
-        @pl.loop(0, n)
+        @pl.loop(0, n, unroll=2)
         def _(child):
             for i in range(lo, hi):
                 problem = tab[i * n + me]
@@ -244,19 +283,13 @@
         first, last = plan.chunks[c]
         return (last - first) * ranks * step
 
-    tile = min(256, width)
-
     def project(c, block, target):
         rows = rows_of(c)
-
-        @pl.loop(0, width // tile)
-        def _(k):
-            here = pl.multiple_of(k * tile, tile)
-            column = pl.multiple_of(block * width + here, tile)
-            value = jnp.dot(
-                r["mixed"][:rows, :], r["wt"][:, pl.ds(column, tile)], preferred_element_type=F32
-            )
-            target[:rows, pl.ds(here, tile)] = value.astype(BF16)
+        column = pl.multiple_of(block * width, width)
+        value = jnp.dot(
+            r["mixed"][:rows, :], r["wt"][:, pl.ds(column, width)], preferred_element_type=F32
+        )
+        target[:rows, :] = value.astype(BF16)
 
     pending = {}
 
@@ -279,73 +312,50 @@
         pending["core", c, hop].start()
         project(c, chip_at(hop) * 2 + my_core, r["own"].at[c % 2, hop])
 
+    opposite = zs // 2
+    ways = (1, zs - 1)
+    piece = 64
+
     def z_copy(c, kind, way):
-        rows = rows_of(c)
-        hop = (1, zs - 1)[way]
+        half = rows_of(c) // 2
+        low = (way if kind == "d" else 1 - way) * half
         if kind == "t":
-            src = r["tsend"].at[pl.ds(way * (rows // 2), rows // 2)]
             dst = r[f"trecv{c}"].at[way]
         else:
-            src = r["dsend"].at[way, pl.ds(0, rows)]
-            dst = r[f"drecv{c}"].at[way]
+            dst = r[f"drecv{c}"].at[way, pl.ds(low, half)]
         return pltpu.make_async_remote_copy(
-            src_ref=src,
+            src_ref=r[kind + "send"].at[way, pl.ds(0, half)],
             dst_ref=dst,
             send_sem=r[kind + "_s"].at[way],
             recv_sem=r[kind + "_r"].at[c, way],
-            device_id=(me, chip_at(hop) * 2 + my_core),
+            device_id=(me, chip_at(ways[way]) * 2 + my_core),
             device_id_type=MESH,
         )
 
-    opposite = zs // 2
-    piece = 32
-
-    def send_far(c):
-        rows = rows_of(c)
-        pending["core", c, opposite].wait_recv()
+    def send_z(c, kind, way):
         if c >= 1:
-            for way in range(2):
-                pending["t", c - 1, way].wait_send()
-
-        @pl.loop(0, rows // piece)
+            pending[kind, c - 1, way].wait_send()
+        half = rows_of(c) // 2
+        hop = opposite if kind == "t" else ways[way]
+        base = (1 - way) * half if kind == "n" else way * half
+
+        @pl.loop(0, half // piece)
         def _(i):
-            at = pl.ds(pl.multiple_of(i * piece, piece), piece)
-            value = r["own"][c % 2, opposite, at, :].astype(F32)
-            value = value + r["crecv"][c % 2, opposite, at, :].astype(F32)
-            r["tsend"][at, :] = value.astype(BF16)
-
+            near = pl.ds(pl.multiple_of(i * piece, piece), piece)
+            at = pl.ds(pl.multiple_of(base + i * piece, piece), piece)
+            value = r["own"][c % 2, hop, at, :].astype(F32)
+            value = value + r["crecv"][c % 2, hop, at, :].astype(F32)
+            if kind == "d":
+                value = value + r[f"trecv{c}"][way, near, :].astype(F32)
+            r[kind + "send"][way, near, :] = value.astype(BF16)
+
+        pending[kind, c, way] = z_copy(c, kind, way)
+        pending[kind, c, way].start()
+
+    def send_through(c):
         for way in range(2):
-            pending["t", c, way] = z_copy(c, "t", way)
-            pending["t", c, way].start()
-
-    def send_near(c):
-        rows = rows_of(c)
-        half = rows // 2
-        for way in range(2):
-            hop = (1, zs - 1)[way]
-            pending["core", c, hop].wait_recv()
             pending["t", c, way].wait_recv()
-            if c >= 1:
-                pending["d", c - 1, way].wait_send()
-
-            @pl.loop(0, half // piece)
-            def _(i):
-                at = pl.ds(pl.multiple_of((1 - way) * half + i * piece, piece), piece)
-                value = r["own"][c % 2, hop, at, :].astype(F32)
-                value = value + r["crecv"][c % 2, hop, at, :].astype(F32)
-                r["dsend"][way, at, :] = value.astype(BF16)
-
-            @pl.loop(0, half // piece)
-            def _(i):
-                start = pl.multiple_of(i * piece, piece)
-                at = pl.ds(pl.multiple_of(way * half + i * piece, piece), piece)
-                value = r["own"][c % 2, hop, at, :].astype(F32)
-                value = value + r["crecv"][c % 2, hop, at, :].astype(F32)
-                value = value + r[f"trecv{c}"][way, pl.ds(start, piece), :].astype(F32)
-                r["dsend"][way, at, :] = value.astype(BF16)
-
-            pending["d", c, way] = z_copy(c, "d", way)
-            pending["d", c, way].start()
+            send_z(c, "d", way)
 
     def square_copy(c, hop):
         return pltpu.make_async_remote_copy(
@@ -361,6 +371,7 @@
         first, last = plan.chunks[c]
         pending["core", c, 0].wait_recv()
         for way in range(2):
+            pending["n", c, way].wait_recv()
             pending["d", c, way].wait_recv()
 
         @pl.loop(0, (last - first) * ranks)
@@ -402,16 +413,23 @@
 
     def project_all(c):
         if c >= 2:
-            finish(c - 2)
             pl.semaphore_wait(r["credit"], 1)
-        hops = [opposite, 1, zs - 1, 0]
-        block_for(c, hops[0])
-        block_for(c, hops[1])
-        send_far(c)
-        block_for(c, hops[2])
-        block_for(c, hops[3])
-
+        block_for(c, opposite)
+        block_for(c, ways[0])
+        pending["core", c, opposite].wait_recv()
+        for way in range(2):
+            send_z(c, "t", way)
+        for way, hop in enumerate((ways[1], 0)):
+            block_for(c, hop)
+            pending["core", c, ways[way]].wait_recv()
+            send_z(c, "n", way)
+
+    loads["kv"].wait()
+    loads["q"].start()
+    loads["fresh"].start()
     spread(0)
+    loads["wt"].start()
+    loads["res"].start()
     if count > 1:
         spread(1)
 
@@ -432,22 +450,26 @@
     fetch(0)
     if count > 2:
         spread(2)
-    for name in ("q", "fresh", "wt", "res"):
-        loads[name].wait()
 
     for c in range(count):
         if c + 1 < count:
             fetch(c + 1)
         if c + 3 < count:
             spread(c + 3)
+        if c >= 1:
+            send_through(c - 1)
         unpack(c)
+        if c == 0:
+            loads["q"].wait()
+            loads["fresh"].wait()
         attend(c)
+        if c == 0:
+            loads["wt"].wait()
+            loads["res"].wait()
+        project_all(c)
         if c >= 1:
-            send_near(c - 1)
-        project_all(c)
-    send_near(count - 1)
-    if count > 1:
-        finish(count - 2)
+            finish(c - 1)
+    send_through(count - 1)
     finish(count - 1)
 
     for c, (first, last) in enumerate(plan.chunks):
@@ -479,7 +501,7 @@
                 scale = r["scale"][j, at, :]
                 for k in range(0, width, LANES):
                     value = r["att"][j, at, k : k + LANES] * scale
-                    value = value * r["gain"][:, k : k + LANES].astype(F32)
+                    value = value * r["gain"][k : k + LANES].astype(F32).reshape(1, LANES)
                     r["res"][slot * problems + problem, low : low + 32, k : k + LANES] = (
                         value.astype(BF16)
                     )
@@ -500,37 +522,13 @@
     for hop in range(zs):
         pending["core", count - 1, hop].wait_send()
     for way in range(2):
-        pending["t", count - 1, way].wait_send()
-        pending["d", count - 1, way].wait_send()
+        for kind in "tnd":
+            pending[kind, count - 1, way].wait_send()
     for c in range(count):
 
         @pl.loop(1, tensor)
         def _(hop):
             square_copy(c, hop).wait_send()
-
-
-def tables(plan, cache_length, parent_device, parent_rank):
-    problems = plan.problems
-    lengths = cache_length.astype(jnp.int32)
-    ids = jnp.arange(problems, dtype=jnp.int32)
-    below = (lengths[None, :] < lengths[:, None]) | (
-        (lengths[None, :] == lengths[:, None]) & (ids[None, :] < ids[:, None])
-    )
-    rank = jnp.sum(below.astype(jnp.int32), axis=1)
-    chosen = (rank[None, :] == ids[:, None]).astype(jnp.int32)
-    order = jnp.sum(chosen * ids[None, :], axis=1)
-    live = jnp.sum(chosen * lengths[None, :], axis=1)
-    used = (lengths + BLK - 1) // BLK
-    start = jnp.sum(jnp.where(rank[None, :] < ids[:, None], used[None, :], 0), axis=1)
-    slot = jnp.arange(plan.slots, dtype=jnp.int32)
-    turn = jnp.sum((start[None, 1:] <= slot[:, None]).astype(jnp.int32), axis=1)
-    mine = (turn[:, None] == ids[None, :]).astype(jnp.int32)
-    problem = jnp.sum(mine * order[None, :], axis=1)
-    block = jnp.clip(slot - jnp.sum(mine * start[None, :], axis=1), 0, plan.blocks - 1)
-    tab = jnp.concatenate([problem, block, order, start, live, rank])
-    wanted = parent_device[:, 0] * plan.ranks + parent_rank
-    req = jnp.zeros((8, LANES), jnp.int32).at[0, : plan.beams].set(wanted)
-    return tab, req
 
 
 def on_device(
@@ -541,7 +539,6 @@
     beams, step, width = queries.shape
     ctx = kv_cache.shape[2]
     plan = Plan(n, tensor, beams, step, ctx, width, cache_length.shape[0], width * tensor)
-    tab, req = tables(plan, cache_length, parent_device, parent_rank)
     count, ranks, most = len(plan.chunks), plan.ranks, plan.row_most
     blocks = kv_cache.reshape(beams, 2, plan.blocks, BLK, HEAD)
 
@@ -549,9 +546,10 @@
     vmem = pl.BlockSpec(memory_space=pltpu.VMEM)
     hbm = pl.BlockSpec(memory_space=pl.ANY)
     inputs = [
-        ("tab", tab, smem),
-        ("req", req, vmem),
-        ("gain", norm_gain.reshape(1, width), vmem),
+        ("length", cache_length, smem),
+        ("device", parent_device.reshape(beams), smem),
+        ("rank", parent_rank, smem),
+        ("gain", norm_gain, vmem),
         ("q_h", queries, hbm),
         ("fresh_h", fresh_kv, hbm),
         ("kv_h", blocks, hbm),
@@ -569,14 +567,17 @@
         ("vbuf", pltpu.VMEM((ranks, plan.rows // BLK, BLK, HEAD), BF16)),
         ("send1", pltpu.VMEM((2, n, ranks, plan.turn_most, 2, BLK, HEAD), BF16)),
         ("send2", pltpu.VMEM((2, n, ranks, plan.turn_most, 2, BLK, HEAD), BF16)),
+        ("tab", pltpu.SMEM((2 * plan.slots + 4 * plan.problems,), jnp.int32)),
+        ("req", pltpu.VMEM((8, LANES), jnp.int32)),
         ("reqv", pltpu.VMEM((n, 8, LANES), jnp.int32)),
         ("reqs", pltpu.SMEM((n, 8, LANES), jnp.int32)),
         ("mixed", pltpu.VMEM((most, width), BF16)),
         ("own", pltpu.VMEM((2, plan.zs, most, width), BF16)),
         ("csend", pltpu.VMEM((plan.zs, most, width), BF16)),
         ("crecv", pltpu.VMEM((2, plan.zs, most, width), BF16)),
-        ("tsend", pltpu.VMEM((most, width), BF16)),
-        ("dsend", pltpu.VMEM((2, most, width), BF16)),
+        ("tsend", pltpu.VMEM((2, most // 2, width), BF16)),
+        ("nsend", pltpu.VMEM((2, most // 2, width), BF16)),
+        ("dsend", pltpu.VMEM((2, most // 2, width), BF16)),
         ("att", pltpu.VMEM((plan.problems, ranks * step, width), F32)),
         ("sums", pltpu.VMEM((most // (ranks * step), ranks * step, LANES), F32)),
         ("scale", pltpu.VMEM((plan.problems, ranks * step, LANES), F32)),
@@ -592,6 +593,8 @@
         ("c_r", dma(count, plan.zs)),
         ("t_s", dma(2)),
         ("t_r", dma(count, 2)),
+        ("n_s", dma(2)),
+        ("n_r", dma(count, 2)),
         ("d_s", dma(2)),
         ("d_r", dma(count, 2)),
         ("s_s", dma(count, tensor)),

time: 146 us -> 128 us (0.88)
  Pallas kernels: 137 us -> 125 us
  other arithmetic: 3.24 us -> 0 us
  local copies, waits for them, and re-layouts: 5.75 us -> 3.14 us
    pallas_call x1, Pallas kernels: 137 us -> 125 us  [on_device(): pl.pallas_call(functools.partial(kernel, plan, names), out_shape=jax.Shap...]
    reduce_sum x4 -> x0, other arithmetic: 1.89 us -> none  [the longest x1 0.91 us: tables(): rank = jnp.sum(below.astype(jnp.int32), axis=1)]
where the time goes in v2:
time: 128 us
  Pallas kernels  125 us (98%)
  local copies, waits for them, and re-layouts  3.14 us (2%)
    pallas_call x1, Pallas kernels, on_device(): pl.pallas_call(functools.partial(kernel, plan, names), out_shape=jax.Shap...  125 us
    unnamed x1, local copies, waits for them, and re-layouts  3.14 us

profile of v2, /device:TPU:1, one launch (start us, length us, event | category | flops | bytes accessed | tf_op | source)
XLA Modules:
  0.0 128.2 jit_solution(7229206330221727078)
XLA Ops:
  0.0 125.0 %step_scoring.1 = bf16[16,64,1024]{2,1,0:T(8,128)(2,1)} custom-call(s32[8]{0:T(128)} %refs_0_.1, s32[16]{0:T(128)} %bitcast.3, s32[16]{0:T(128)} %refs_2_.1, bf16[1024]{0:T(1024)(128)(2,1)} %refs_3_.1, bf16[16,64,1024]{2,1,0:T(8,128)(2,1)} %refs_4_.1, bf16[16,2,64,128]{3,2,1,0:T(8,128)(2,1)} %refs_5_.1, bf16[16,2,32,16,128]{4,3,2,1,0:T(8,128)(2,1)} %bitcast.2, ...), custom_call_target="tpu_custom_call" | custom-call | flops 19595788288 | bytes 31457280 | tf_op jit(solution)/shard_map/step_scoring/pallas_call | solution.py:618
  125.0 3.1 %copy.11 = bf16[16,64,1024]{2,1,0:T(8,128)(2,1)} copy(bf16[16,64,1024]{2,1,0:T(8,128)(2,1)} %step_scoring.1) | data formatting | bytes 4194304

commit v3 on v2

--- a/solution.py
+++ b/solution.py
@@ -16,6 +16,7 @@
 F32 = jnp.float32
 BF16 = jnp.bfloat16
 STRIDE = 7
+MIX = (1, 4, 3, 12, 6, 9, 14, 11, 5, 15, 7, 13, 10, 2, 8)
 
 
 class Plan:
@@ -62,21 +63,31 @@
     slots = plan.slots
     me = lax.axis_index("dp")
     mine = lax.axis_index("tensor")
-    my_y, my_x = me // side, me % side
-    my_z, my_core = mine // 2, mine % 2
+
+    def div(a, b):
+        return lax.div(a, jnp.int32(b))
+
+    def rem(a, b):
+        return lax.rem(a, jnp.int32(b))
+
+    my_y, my_x = div(me, side), rem(me, side)
+    my_z, my_core = div(mine, 2), rem(mine, 2)
     tab, reqs = r["tab"], r["reqs"]
     at_order, at_off, at_len, at_rank = (2 * slots + problems * i for i in range(4))
 
     def plane_peer(index):
-        hop = (index * STRIDE) % n
-        there = ((my_y + hop // side) % side) * side + (my_x + hop % side) % side
+        if isinstance(index, int):
+            hop = MIX[index - 1] if n == 16 else index
+            return hop, rem(my_y + hop // side, side) * side + rem(my_x + hop % side, side)
+        hop = rem(index * STRIDE, n)
+        there = rem(my_y + div(hop, side), side) * side + rem(my_x + rem(hop, side), side)
         return hop, there
 
     def tensor_peer(hop):
-        return (mine + hop) % tensor
+        return rem(mine + hop, tensor)
 
     def chip_at(hop):
-        return (my_z + hop) % zs
+        return rem(my_z + hop, zs)
 
     barrier = pltpu.get_barrier_semaphore()
 
@@ -119,7 +130,7 @@
         starts.append(start)
 
     def place(lo, hi):
-        @pl.loop(lo * n, hi * n)
+        @pl.loop(lo * n, hi * n, unroll=4)
         def _(slot):
             turn = jnp.int32(0)
             for j in range(1, problems):
@@ -134,8 +145,6 @@
         value = r["device"][b] * ranks + r["rank"][b]
         wanted = jnp.where(lane == b, value, wanted)
     r["req"][...] = wanted
-
-    pl.semaphore_wait(barrier, n - 1 + tensor - 1)
 
     def request_copy(index):
         hop, there = plane_peer(index)
@@ -148,18 +157,14 @@
             device_id_type=MESH,
         )
 
-    @pl.loop(1, n)
-    def _(index):
-        request_copy(index).start()
-
     r["reqv"][me] = r["req"][...]
 
     def spread_copy(c, index):
         hop, there = plane_peer(index)
         lo, hi = plan.turns[c]
         return pltpu.make_async_remote_copy(
-            src_ref=r["send1"].at[c % 2, there, pl.ds(0, ranks), pl.ds(0, hi - lo)],
-            dst_ref=r[f"stash{c}"].at[pl.ds(me * ranks, ranks)],
+            src_ref=r["send1"].at[c % 2, there, pl.ds(0, ranks * (hi - lo))],
+            dst_ref=r[f"stash{c}"].at[pl.ds(me * (ranks * (hi - lo)), ranks * (hi - lo))],
             send_sem=r["p1_s"].at[c, hop],
             recv_sem=r["p1_r"].at[c, hop],
             device_id=(there, mine),
@@ -170,7 +175,7 @@
         hop, there = plane_peer(index)
         lo, hi = plan.turns[c]
         return pltpu.make_async_remote_copy(
-            src_ref=r["send2"].at[c % 2, there, pl.ds(0, ranks), pl.ds(0, hi - lo)],
+            src_ref=r["send2"].at[c % 2, there, pl.ds(0, ranks * (hi - lo))],
             dst_ref=r[f"got{c}"].at[me],
             send_sem=r["p2_s"].at[c, hop],
             recv_sem=r["p2_r"].at[c, hop],
@@ -179,11 +184,10 @@
         )
 
     def each_peer(make, c, what):
-        @pl.loop(1, n)
-        def _(index):
+        for index in range(1, n):
             getattr(make(c, index), what)()
 
-    def spread(c):
+    def pack(c):
         lo, hi = plan.turns[c]
         place(lo, hi)
         if c >= 2:
@@ -195,13 +199,15 @@
                 problem = tab[i * n + k]
                 block = tab[slots + i * n + k]
                 for rank in range(ranks):
-                    r["send1"][c % 2, k, rank, i - lo] = r["kv"][
+                    r["send1"][c % 2, k, rank * (hi - lo) + i - lo] = r["kv"][
                         rank * problems + problem, :, block
                     ]
 
+    def spread(c):
+        lo, hi = plan.turns[c]
         each_peer(spread_copy, c, "start")
-        for rank in range(ranks):
-            r[f"stash{c}"][me * ranks + rank] = r["send1"][c % 2, me, rank, : hi - lo]
+        for k in range(ranks * (hi - lo)):
+            r[f"stash{c}"][me * (ranks * (hi - lo)) + k] = r["send1"][c % 2, me, k]
 
     def fetch(c):
         lo, hi = plan.turns[c]
@@ -215,10 +221,12 @@
                 problem = tab[i * n + me]
                 for slot in range(ranks):
                     parent = reqs[child, 0, slot * problems + problem]
-                    r["send2"][c % 2, child, slot, i - lo] = r[f"stash{c}"][parent, i - lo]
+                    r["send2"][c % 2, child, slot * (hi - lo) + i - lo] = r[f"stash{c}"][
+                        parent * (hi - lo) + i - lo
+                    ]
 
         each_peer(fetch_copy, c, "start")
-        r[f"got{c}"][me] = r["send2"][c % 2, me, :, : hi - lo]
+        r[f"got{c}"][me] = r["send2"][c % 2, me, : ranks * (hi - lo)]
 
     def unpack(c):
         lo, hi = plan.turns[c]
@@ -229,7 +237,9 @@
             for i in range(lo, hi):
                 for slot in range(ranks):
                     for part, name in enumerate(("kbuf", "vbuf")):
-                        r[name][slot, i * n + k] = r[f"got{c}"][k, slot, i - lo, part]
+                        r[name][slot, i * n + k] = r[f"got{c}"][
+                            k, slot * (hi - lo) + i - lo, part
+                        ]
 
     group = min(4, heads)
     factor = math.log2(math.e) / math.sqrt(HEAD)
@@ -427,10 +437,18 @@
     loads["kv"].wait()
     loads["q"].start()
     loads["fresh"].start()
+    pack(0)
+    pl.semaphore_wait(barrier, n - 1 + tensor - 1)
     spread(0)
+
+    @pl.loop(1, n)
+    def _(index):
+        request_copy(index).start()
+
     loads["wt"].start()
     loads["res"].start()
     if count > 1:
+        pack(1)
         spread(1)
 
     @pl.loop(1, n)
@@ -449,12 +467,14 @@
     table.wait()
     fetch(0)
     if count > 2:
+        pack(2)
         spread(2)
 
     for c in range(count):
         if c + 1 < count:
             fetch(c + 1)
         if c + 3 < count:
+            pack(c + 3)
             spread(c + 3)
         if c >= 1:
             send_through(c - 1)
@@ -529,6 +549,23 @@
         @pl.loop(1, tensor)
         def _(hop):
             square_copy(c, hop).wait_send()
+
+
+PIECES = 4
+
+
+def hand_over(source, target, held, in_sem, out_sem):
+    size = source.shape[0] // PIECES
+    for i in range(PIECES):
+        at = pl.ds(i * size, size)
+        pltpu.make_async_copy(source.at[at], held.at[at], in_sem.at[i]).start()
+    for i in range(PIECES):
+        at = pl.ds(i * size, size)
+        pltpu.make_async_copy(source.at[at], held.at[at], in_sem.at[i]).wait()
+        pltpu.make_async_copy(held.at[at], target.at[at], out_sem.at[i]).start()
+    for i in range(PIECES):
+        at = pl.ds(i * size, size)
+        pltpu.make_async_copy(held.at[at], target.at[at], out_sem.at[i]).wait()
 
 
 def on_device(
@@ -565,8 +602,8 @@
         ("res", pltpu.VMEM(residual.shape, BF16)),
         ("kbuf", pltpu.VMEM((ranks, plan.rows // BLK, BLK, HEAD), BF16)),
         ("vbuf", pltpu.VMEM((ranks, plan.rows // BLK, BLK, HEAD), BF16)),
-        ("send1", pltpu.VMEM((2, n, ranks, plan.turn_most, 2, BLK, HEAD), BF16)),
-        ("send2", pltpu.VMEM((2, n, ranks, plan.turn_most, 2, BLK, HEAD), BF16)),
+        ("send1", pltpu.VMEM((2, n, ranks * plan.turn_most, 2, BLK, HEAD), BF16)),
+        ("send2", pltpu.VMEM((2, n, ranks * plan.turn_most, 2, BLK, HEAD), BF16)),
         ("tab", pltpu.SMEM((2 * plan.slots + 4 * plan.problems,), jnp.int32)),
         ("req", pltpu.VMEM((8, LANES), jnp.int32)),
         ("reqv", pltpu.VMEM((n, 8, LANES), jnp.int32)),
@@ -606,8 +643,8 @@
         (first, last), (lo, hi) = plan.chunks[c], plan.turns[c]
         rows = (last - first) * ranks * step
         scratch += [
-            (f"stash{c}", pltpu.VMEM((n * ranks, hi - lo, 2, BLK, HEAD), BF16)),
-            (f"got{c}", pltpu.VMEM((n, ranks, hi - lo, 2, BLK, HEAD), BF16)),
+            (f"stash{c}", pltpu.VMEM((n * ranks * (hi - lo), 2, BLK, HEAD), BF16)),
+            (f"got{c}", pltpu.VMEM((n, ranks * (hi - lo), 2, BLK, HEAD), BF16)),
             (f"trecv{c}", pltpu.VMEM((2, rows // 2, width), BF16)),
             (f"drecv{c}", pltpu.VMEM((2, rows, width), BF16)),
             (f"sq{c}", pltpu.VMEM((last - first, 8, ranks * step), F32)),
@@ -615,7 +652,7 @@
         ]
     names = [i[0] for i in inputs] + ["out_h"] + [s[0] for s in scratch]
     rows = beams * step
-    return pl.pallas_call(
+    scored = pl.pallas_call(
         functools.partial(kernel, plan, names),
         out_shape=jax.ShapeDtypeStruct(residual.shape, BF16),
         in_specs=[i[2] for i in inputs],
@@ -631,6 +668,18 @@
         ),
         name="step_scoring",
     )(*[i[1] for i in inputs])
+    return pl.pallas_call(
+        hand_over,
+        out_shape=jax.ShapeDtypeStruct(residual.shape, BF16),
+        in_specs=[hbm],
+        out_specs=hbm,
+        scratch_shapes=[
+            pltpu.VMEM(residual.shape, BF16),
+            pltpu.SemaphoreType.DMA((PIECES,)),
+            pltpu.SemaphoreType.DMA((PIECES,)),
+        ],
+        name="hand_over",
+    )(scored)
 
 
 def solution(mesh):

time: 128 us -> 128 us (level)
  local copies, waits for them, and re-layouts: 3.14 us -> 0 us
  Pallas kernels: 125 us -> 127 us
    unnamed x1 -> x0, local copies, waits for them, and re-layouts: 3.14 us -> none
    pallas_call x0 -> x1, Pallas kernels: none -> 2.42 us  [on_device(): pl.pallas_call(hand_over, out_shape=jax.ShapeDtypeStruct(residual.shape,...]
where the time goes in v3:
time: 128 us; the launch traced here: 127 us
  Pallas kernels  127 us (99%)
    pallas_call x1, Pallas kernels, on_device(): pl.pallas_call(functools.partial(kernel, plan, names), out_shape=jax.Shap...  125 us

profile of v3, /device:TPU:1, one launch (start us, length us, event | category | flops | bytes accessed | tf_op | source)
XLA Modules:
  0.0 127.4 jit_solution(15486328251240769241)
XLA Ops:
  0.0 124.8 %step_scoring.1.source = bf16[16,64,1024]{2,1,0:T(8,128)(2,1)} custom-call(s32[8]{0:T(128)} %refs_0_.1, s32[16]{0:T(128)} %bitcast.3, s32[16]{0:T(128)} %refs_2_.1, bf16[1024]{0:T(1024)(128)(2,1)} %refs_3_.1, bf16[16,64,1024]{2,1,0:T(8,128)(2,1)} %refs_4_.1, bf16[16,2,64,128]{3,2,1,0:T(8,128)(2,1)} %refs_5_.1, bf16[16,2,32,16,128]{4,3,2,1,0:T(8,128)(2,1)} %bitcast.2, ...), custom_call_target="tpu_custom_call" | custom-call | flops 19595788288 | bytes 31457280 | tf_op jit(solution)/shard_map/step_scoring/pallas_call | solution.py:655
  124.8 2.4 %hand_over.1 = bf16[16,64,1024]{2,1,0:T(8,128)(2,1)} custom-call(bf16[16,64,1024]{2,1,0:T(8,128)(2,1)} %step_scoring.1.source), custom_call_target="tpu_custom_call" | custom-call | tf_op jit(solution)/shard_map/hand_over/pallas_call | solution.py:671
